TPU v7x, 32 devices: a whole 2x2x4 slice. The times are simulated.
32 devices in a mesh: groups: 2 (over y), row: 4 (over z), tm: 2 (over x), chan: 2 (over core).
Axes of the slice: x: 2, y: 2, z: 4, core: 2. Of those that a mesh axis runs over, the one named last changes fastest.
Arguments:
- field_in: bfloat16 [64, 8, 128, 128], P(('groups', 'row'), 'tm', 'chan'), parts along dimension 0, may hold values from -6 to 6
- spectral_weight: bfloat16 [8, 32, 32, 2, 128, 128], P('tm', 'row', None, None, 'chan'), may hold values from -0.75 to 0.75
- conv_weight: bfloat16 [128, 128], P('chan'), may hold values from -0.5 to 0.5
- conv_bias: float32 [128], P('chan'), may hold values from -3 to 3
Outputs:
- layer_out: bfloat16 [64, 8, 128, 128], P(('groups', 'row'), 'tm', 'chan'), parts along dimension 0
There are 2 independent parts, one for each index of `groups`. A program takes and returns all parts, laid end to end along the dimension named above; an argument that names none is the same for every part. Nothing has to cross between parts.
All inputs are finite; a program needn't handle non-finite values.
Results may differ from a plain program's by a relative error of at most 0.007.
Values may be sent and summed in bfloat16 or wider, within the bound.
A program may use at most 128 MiB of HBM per device.

v0:
```python
import functools

import jax
import jax.numpy as jnp
import numpy as np
from jax import lax
from jax.experimental import pallas as pl
from jax.experimental.pallas import tpu as pltpu
from jax.sharding import PartitionSpec as P

MESH = pl.DeviceIdType.MESH
F32 = jnp.float32
BF16 = jnp.bfloat16


def angles(frequency, position, period):
    return 2.0 * np.pi * np.mod(np.outer(frequency, position), period) / period


def signed(count):
    index = np.arange(count)
    return np.where(index < count // 2, index, index - count)


def swap_halves(value):
    return pltpu.roll(value, 64, axis=value.ndim - 1)


def kernel(
    dims,
    field,
    weights,
    conv_w,
    bias,
    x_fwd,
    x_inv,
    tab_y,
    tab_t,
    out,
    w_all,
    f_all,
    sect,
    sect_s,
    y_send,
    y_recv,
    own_kt,
    t_send,
    t_recv,
    coef,
    modes,
    back,
    acc,
    conv,
    w_sem,
    f_sem,
    fs_sem,
    fr_sem,
    ys_sem,
    yr_sem,
    ts_sem,
    tr_sem,
    cs_sem,
    cr_sem,
    ms_sem,
    mr_sem,
    bs_sem,
    br_sem,
):
    rows, slabs, yd, td, kyd, ktd, kx = dims
    ky_all, kt_all = rows * kyd, slabs * ktd
    row, tm, chan = lax.axis_index("row"), lax.axis_index("tm"), lax.axis_index("chan")
    y0, t0 = row * yd, tm * td
    half = 64

    barrier = pltpu.get_barrier_semaphore()
    for d in range(1, rows):
        pl.semaphore_signal(
            barrier, inc=1, device_id={"row": lax.rem(row + d, rows)}, device_id_type=MESH
        )
    for d in range(1, slabs):
        pl.semaphore_signal(
            barrier, inc=1, device_id={"tm": lax.rem(tm + d, slabs)}, device_id_type=MESH
        )
    pl.semaphore_signal(barrier, inc=1, device_id={"chan": 1 - chan}, device_id_type=MESH)

    mine = pl.ds(pl.multiple_of(chan * half, half), half)
    own_field = pltpu.make_async_copy(field, f_all.at[:, mine, :], f_sem)
    own_field.start()
    w_copies = [
        pltpu.make_async_copy(weights.at[b], w_all.at[b], w_sem.at[b]) for b in range(ktd)
    ]
    for copy in w_copies:
        copy.start()

    lane = lax.broadcasted_iota(jnp.int32, (kx, 128), 1)
    low = lane < half
    sgn_f = jnp.where(low, 1.0, -1.0).astype(F32)
    low8 = low[:8]
    sgn_b = -sgn_f

    own_field.wait()

    def x_step(i, carry):
        block = f_all[pl.ds(2 * i, 2), mine, :].reshape(2 * half, 128)
        both = lax.dot_general(
            x_fwd[...], block, (((1,), (1,)), ((), ())), preferred_element_type=F32
        )
        re, im = both[:kx], both[kx:]
        first = jnp.where(low, re, swap_halves(im))
        second = jnp.where(low, swap_halves(re), im)
        sect[2 * i] = first
        sect_s[2 * i] = swap_halves(first) * sgn_f
        sect[2 * i + 1] = second
        sect_s[2 * i + 1] = swap_halves(second) * sgn_f
        return carry

    lax.fori_loop(0, yd * td // 2, x_step, 0)

    pl.semaphore_wait(barrier, rows - 1 + slabs - 1 + 1)
    pending = []

    y_recvs = []
    for d in list(range(1, rows)) + [0]:
        dest = lax.rem(row + d, rows)

        def y_step(a, carry, d=d, dest=dest):
            k = dest * kyd + a
            for t in range(td):
                total = jnp.zeros((kx, 128), F32)
                for y in range(yd):
                    total += tab_y[k, y0 + y] * sect[y * td + t]
                    total += tab_y[ky_all + k, y0 + y] * sect_s[y * td + t]
                if d == 0:
                    y_recv[row, a, t] = total.astype(BF16)
                else:
                    y_send[d - 1, a, t] = total.astype(BF16)
            return carry

        lax.fori_loop(0, kyd, y_step, 0)
        if d > 0:
            copy = pltpu.make_async_remote_copy(
                src_ref=y_send.at[d - 1],
                dst_ref=y_recv.at[row],
                send_sem=ys_sem.at[d - 1],
                recv_sem=yr_sem.at[d - 1],
                device_id={"row": dest},
                device_id_type=MESH,
            )
            copy.start()
            pending.append(copy)
            y_recvs.append(copy)

    f_copy = pltpu.make_async_remote_copy(
        src_ref=field,
        dst_ref=f_all.at[:, mine, :],
        send_sem=fs_sem,
        recv_sem=fr_sem,
        device_id={"chan": 1 - chan},
        device_id_type=MESH,
    )
    f_copy.start()
    pending.append(f_copy)
    f_copy.wait_recv()

    def conv_step(i, carry):
        conv[i] = jnp.dot(conv_w[...], f_all[i], preferred_element_type=F32) + bias[...]
        return carry

    lax.fori_loop(0, yd * td, conv_step, 0)

    for copy in y_recvs:
        copy.wait_recv()

    def t_step(a, carry):
        parts = []
        for t in range(td):
            total = y_recv[0, a, t].astype(F32)
            for r in range(1, rows):
                total += y_recv[r, a, t].astype(F32)
            parts.append((total, swap_halves(total) * sgn_f))
        for d in range(slabs):
            dest = lax.rem(tm + d, slabs)
            for b in range(ktd):
                k = dest * ktd + b
                value = jnp.zeros((kx, 128), F32)
                for t in range(td):
                    value += tab_t[k, t0 + t] * parts[t][0]
                    value += tab_t[kt_all + k, t0 + t] * parts[t][1]
                if d == 0:
                    own_kt[b, a] = value
                else:
                    t_send[d - 1, b, a] = value.astype(BF16)
        return carry

    lax.fori_loop(0, kyd, t_step, 0)
    t_copies = []
    for d in range(1, slabs):
        copy = pltpu.make_async_remote_copy(
            src_ref=t_send.at[d - 1],
            dst_ref=t_recv.at[d - 1],
            send_sem=ts_sem.at[d - 1],
            recv_sem=tr_sem.at[d - 1],
            device_id={"tm": lax.rem(tm + d, slabs)},
            device_id_type=MESH,
        )
        copy.start()
        t_copies.append(copy)
        pending.append(copy)
    for copy in t_copies:
        copy.wait_recv()

    for b in range(ktd):

        def c_step(a, carry, b=b):
            value = own_kt[b, a]
            for d in range(1, slabs):
                value += t_recv[d - 1, b, a].astype(F32)
            coef[chan, b, a] = value.astype(BF16)
            return carry

        lax.fori_loop(0, kyd, c_step, 0)
    c_copy = pltpu.make_async_remote_copy(
        src_ref=coef.at[chan],
        dst_ref=coef.at[chan],
        send_sem=cs_sem,
        recv_sem=cr_sem,
        device_id={"chan": 1 - chan},
        device_id_type=MESH,
    )
    c_copy.start()
    pending.append(c_copy)
    c_copy.wait_recv()

    group = 8 * 2 * half
    sub = lax.broadcasted_iota(jnp.int32, (8, 128), 0)
    zero = jnp.zeros((8, 128), F32)
    m_copies = []
    for b in range(ktd):
        w_copies[b].wait()
        kt = tm * ktd + b

        def mix_step(a, carry, b=b, kt=kt):
            left = coef[0, b, a].astype(F32)
            right = coef[1, b, a].astype(F32)
            re = jnp.where(low, left, swap_halves(right))
            im = jnp.where(low, swap_halves(left), right)
            pieces = []
            for g in range(0, kx // 8, 2):
                first, second = slice(8 * g, 8 * g + 8), slice(8 * g + 8, 8 * g + 16)
                lhs = jnp.concatenate(
                    [
                        jnp.concatenate([re[first], zero], axis=1),
                        jnp.concatenate([im[first], zero], axis=1),
                        jnp.concatenate([zero, re[second]], axis=1),
                        jnp.concatenate([zero, im[second]], axis=1),
                    ],
                    axis=0,
                ).astype(BF16)
                rhs = jnp.concatenate(
                    [
                        w_all[b, a, g * group : (g + 1) * group, :],
                        w_all[b, a, (g + 1) * group : (g + 2) * group, :],
                    ],
                    axis=1,
                )
                result = lax.dot_general(
                    lhs, rhs, (((1,), (1,)), ((), ())), preferred_element_type=F32
                )
                for h in range(2):
                    by_part = []
                    for p in range(2):
                        tile = result[16 * h + 8 * p : 16 * h + 8 * p + 8]
                        total = tile[:, :128]
                        for m in range(1, 8):
                            total = jnp.where(sub == m, tile[:, 128 * m : 128 * m + 128], total)
                        by_part.append(total)
                    turned = swap_halves(by_part[1])
                    pieces.append(by_part[0] + jnp.where(low8, -turned, turned))
            modes[kt, a] = jnp.concatenate(pieces, axis=0).astype(BF16)
            return carry

        lax.fori_loop(0, kyd, mix_step, 0)
        for d in range(1, slabs):
            copy = pltpu.make_async_remote_copy(
                src_ref=modes.at[kt],
                dst_ref=modes.at[kt],
                send_sem=ms_sem.at[d - 1, b],
                recv_sem=mr_sem.at[d - 1, b],
                device_id={"tm": lax.rem(tm + d, slabs)},
                device_id_type=MESH,
            )
            copy.start()
            m_copies.append(copy)
            pending.append(copy)
    for copy in m_copies:
        copy.wait_recv()

    def bt_step(a, carry):
        totals = [jnp.zeros((kx, 128), F32) for _ in range(td)]
        for k in range(kt_all):
            value = modes[k, a].astype(F32)
            turned = swap_halves(value) * sgn_b
            for t in range(td):
                totals[t] += tab_t[k, t0 + t] * value + tab_t[kt_all + k, t0 + t] * turned
        for t in range(td):
            back[row, a, t] = totals[t].astype(BF16)
        return carry

    lax.fori_loop(0, kyd, bt_step, 0)
    b_copies = []
    for d in range(1, rows):
        copy = pltpu.make_async_remote_copy(
            src_ref=back.at[row],
            dst_ref=back.at[row],
            send_sem=bs_sem.at[d - 1],
            recv_sem=br_sem.at[d - 1],
            device_id={"row": lax.rem(row + d, rows)},
            device_id_type=MESH,
        )
        copy.start()
        b_copies.append(copy)
        pending.append(copy)

    for d in range(rows):
        source = lax.rem(row - d + rows, rows)
        if d > 0:
            b_copies[d - 1].wait_recv()

        def by_step(t, carry, d=d, source=source):
            if d == 0:
                totals = [jnp.zeros((kx, 128), F32) for _ in range(yd)]
            else:
                totals = [acc[y * td + t] for y in range(yd)]
            for a in range(kyd):
                k = source * kyd + a
                value = back[source, a, t].astype(F32)
                turned = swap_halves(value) * sgn_b
                for y in range(yd):
                    totals[y] += (
                        tab_y[k, y0 + y] * value + tab_y[ky_all + k, y0 + y] * turned
                    )
            for y in range(yd):
                acc[y * td + t] = totals[y]
            return carry

        lax.fori_loop(0, td, by_step, 0)

    def out_step(i, carry):
        first, second = acc[2 * i], acc[2 * i + 1]
        both = jnp.concatenate(
            [
                jnp.where(low, first, swap_halves(second)),
                jnp.where(low, swap_halves(first), second),
            ],
            axis=0,
        )
        spectral = jnp.dot(both.T.astype(BF16), x_inv[...], preferred_element_type=F32)
        value = spectral + conv[pl.ds(2 * i, 2)].reshape(2 * half, 128)
        value = 0.5 * value * (1.0 + lax.erf(value * np.float32(1.0 / np.sqrt(2.0))))
        out[pl.ds(2 * i, 2)] = value.astype(BF16).reshape(2, half, 128)
        return carry

    lax.fori_loop(0, yd * td // 2, out_step, 0)
    for copy in pending:
        copy.wait_send()


def body(field_in, spectral_weight, conv_weight, conv_bias):
    yd, td, half, nx = field_in.shape
    ktd, kyd, kx = spectral_weight.shape[:3]
    out_c, in_c = spectral_weight.shape[4:]
    rows, slabs = lax.axis_size("row"), lax.axis_size("tm")
    ny, nt = yd * rows, td * slabs
    ky_all, kt_all = kyd * rows, ktd * slabs

    turn_x = angles(np.arange(kx), np.arange(nx), nx)
    x_fwd = jnp.asarray(np.concatenate([np.cos(turn_x), -np.sin(turn_x)], axis=0), BF16)
    scale = (np.where(np.arange(kx) == 0, 1.0, 2.0) / (nx * ny * nt))[:, None]
    x_inv = jnp.asarray(
        np.concatenate([np.cos(turn_x) * scale, -np.sin(turn_x) * scale], axis=0), BF16
    )
    turn_y = angles(signed(ky_all), np.arange(ny), ny)
    tab_y = jnp.asarray(np.concatenate([np.cos(turn_y), np.sin(turn_y)], axis=0), F32)
    turn_t = angles(signed(kt_all), np.arange(nt), nt)
    tab_t = jnp.asarray(np.concatenate([np.cos(turn_t), np.sin(turn_t)], axis=0), F32)

    dims = (rows, slabs, yd, td, kyd, ktd, kx)
    vmem = pl.BlockSpec(memory_space=pltpu.VMEM)
    smem = pl.BlockSpec(memory_space=pltpu.SMEM)
    hbm = pl.BlockSpec(memory_space=pl.ANY)
    dma = pltpu.SemaphoreType.DMA
    tile = (kx, 128)
    result = pl.pallas_call(
        functools.partial(kernel, dims),
        out_shape=jax.ShapeDtypeStruct((yd * td, half, nx), BF16),
        in_specs=[hbm, hbm, vmem, vmem, vmem, vmem, smem, smem],
        out_specs=vmem,
        scratch_shapes=[
            pltpu.VMEM((ktd, kyd, kx * 2 * out_c, in_c), BF16),
            pltpu.VMEM((yd * td, in_c, nx), BF16),
            pltpu.VMEM((yd * td,) + tile, F32),
            pltpu.VMEM((yd * td,) + tile, F32),
            pltpu.VMEM((rows - 1, kyd, td) + tile, BF16),
            pltpu.VMEM((rows, kyd, td) + tile, BF16),
            pltpu.VMEM((ktd, kyd) + tile, F32),
            pltpu.VMEM((slabs - 1, ktd, kyd) + tile, BF16),
            pltpu.VMEM((slabs - 1, ktd, kyd) + tile, BF16),
            pltpu.VMEM((2, ktd, kyd) + tile, BF16),
            pltpu.VMEM((kt_all, kyd) + tile, BF16),
            pltpu.VMEM((rows, kyd, td) + tile, BF16),
            pltpu.VMEM((yd * td,) + tile, F32),
            pltpu.VMEM((yd * td, out_c, nx), F32),
            dma((ktd,)),
            dma,
            dma,
            dma,
            dma((rows - 1,)),
            dma((rows - 1,)),
            dma((slabs - 1,)),
            dma((slabs - 1,)),
            dma,
            dma,
            dma((slabs - 1, ktd)),
            dma((slabs - 1, ktd)),
            dma((rows - 1,)),
            dma((rows - 1,)),
        ],
        compiler_params=pltpu.CompilerParams(
            collective_id=0, has_side_effects=True, vmem_limit_bytes=56 * 1024 * 1024
        ),
    )(
        field_in.reshape(yd * td, half, nx),
        spectral_weight.reshape(ktd, kyd, kx * 2 * out_c, in_c),
        conv_weight,
        conv_bias[:, None],
        x_fwd,
        x_inv,
        tab_y,
        tab_t,
    )
    return result.reshape(yd, td, half, nx)


def solution(mesh):
    return jax.shard_map(
        body,
        mesh=mesh,
        in_specs=(
            P(("groups", "row"), "tm", "chan", None),
            P("tm", "row", None, None, "chan", None),
            P("chan", None),
            P("chan"),
        ),
        out_specs=P(("groups", "row"), "tm", "chan", None),
        check_vma=False,
    )
```

profile of v0, /device:TPU:25, one launch (start us, length us, event | category | flops | bytes accessed | tf_op | source)
XLA Modules:
  0.0 105.8 jit_solution(8054763237829765992)
XLA Ops:
  0.0 1.4 %copy.9.bias = f32[64,1]{1,0:T(8,128)} copy(f32[64,1]{0,1:T(1,128)} %bitcast.7) | data formatting | bytes 512 | tf_op jit(solution)/shard_map/broadcast_in_dim | solution.py:435
  1.4 102.5 %shard_map.82 = bf16[32,64,128]{2,1,0:T(8,128)(2,1)} custom-call(bf16[32,64,128]{2,1,0:T(8,128)(2,1)} %bitcast.6, bf16[4,8,4096,128]{3,2,1,0:T(8,128)(2,1)} %bitcast.4, bf16[64,128]{1,0:T(8,128)(2,1)} %conv_w.1, f32[64,1]{1,0:T(8,128)} %copy.9.bias, bf16[64,128]{1,0:T(8,128)(2,1)} %constant.8.clone.x_fwd, bf16[64,128]{1,0:T(8,128)(2,1)} %constant.9.clone.x_inv, ...), custom_call_target="tpu_custom_call" | custom-call | tf_op jit(solution)/shard_map/pallas_call | solution.py:393
  103.9 1.9 %copy.11 = bf16[8,4,64,128]{3,2,1,0:T(8,128)(2,1)} copy(bf16[8,4,64,128]{3,2,1,0:T(8,128)(2,1)} %bitcast.5) | data formatting | bytes 1048576
where the time goes:
time: 106 us
  Pallas kernels  103 us (97%)
  local copies, waits for them, and re-layouts  3.23 us (3%)
    pallas_call x1, Pallas kernels, body(): pl.pallas_call(functools.partial(kernel, dims), out_shape=jax.ShapeDtypeS...  103 us

commit v1 on v0

v1 whole, which is shorter than its diff:
```python
import functools

import jax
import jax.numpy as jnp
import numpy as np
from jax import lax
from jax.experimental import pallas as pl
from jax.experimental.pallas import tpu as pltpu
from jax.sharding import PartitionSpec as P

MESH = pl.DeviceIdType.MESH
F32 = jnp.float32
BF16 = jnp.bfloat16


def angles(frequency, position, period):
    return 2.0 * np.pi * np.mod(np.outer(frequency, position), period) / period


def signed(count):
    index = np.arange(count)
    return np.where(index < count // 2, index, index - count)


def swap_halves(value):
    return pltpu.roll(value, 64, axis=value.ndim - 1)


def kernel(
    dims,
    field,
    weights,
    conv_w,
    bias,
    x_fwd,
    x_inv,
    tab_y,
    tab_t,
    out,
    w_all,
    f_all,
    sect,
    sect_s,
    y_send,
    y_recv,
    own_kt,
    t_send,
    t_recv,
    coef,
    modes,
    back,
    acc,
    conv,
    w_sem,
    f_sem,
    fs_sem,
    fr_sem,
    ys_sem,
    yr_sem,
    ts_sem,
    tr_sem,
    cs_sem,
    cr_sem,
    ms_sem,
    mr_sem,
    bs_sem,
    br_sem,
):
    rows, slabs, yd, td, kyd, ktd, kx, parts = dims
    ky_all, kt_all = rows * kyd, slabs * ktd
    row, tm, chan = lax.axis_index("row"), lax.axis_index("tm"), lax.axis_index("chan")
    y0, t0 = row * yd, tm * td
    half = 64

    barrier = pltpu.get_barrier_semaphore()
    for d in range(1, rows):
        pl.semaphore_signal(
            barrier, inc=1, device_id={"row": lax.rem(row + d, rows)}, device_id_type=MESH
        )
    for d in range(1, slabs):
        pl.semaphore_signal(
            barrier, inc=1, device_id={"tm": lax.rem(tm + d, slabs)}, device_id_type=MESH
        )
    pl.semaphore_signal(barrier, inc=1, device_id={"chan": 1 - chan}, device_id_type=MESH)

    mine = pl.ds(pl.multiple_of(chan * half, half), half)
    own_field = pltpu.make_async_copy(field, f_all.at[:, mine, :], f_sem)
    own_field.start()
    span = max(1, kyd // parts)
    count = kyd // span
    part = [pl.ds(c * span, span) for c in range(count)]
    w_copies = [
        pltpu.make_async_copy(weights.at[:, part[c]], w_all.at[:, part[c]], w_sem.at[c])
        for c in range(count)
    ]
    for copy in w_copies:
        copy.start()

    lane = lax.broadcasted_iota(jnp.int32, (kx, 128), 1)
    low = lane < half
    sgn_f = jnp.where(low, 1.0, -1.0).astype(F32)
    low8 = low[:8]
    sgn_b = -sgn_f

    own_field.wait()

    def x_step(i, carry):
        block = f_all[pl.ds(2 * i, 2), mine, :].reshape(2 * half, 128)
        both = lax.dot_general(
            x_fwd[...], block, (((1,), (1,)), ((), ())), preferred_element_type=F32
        )
        re, im = both[:kx], both[kx:]
        first = jnp.where(low, re, swap_halves(im))
        second = jnp.where(low, swap_halves(re), im)
        sect[2 * i] = first
        sect_s[2 * i] = swap_halves(first) * sgn_f
        sect[2 * i + 1] = second
        sect_s[2 * i + 1] = swap_halves(second) * sgn_f
        return carry

    lax.fori_loop(0, yd * td // 2, x_step, 0)

    pl.semaphore_wait(barrier, rows - 1 + slabs - 1 + 1)
    pending = []

    def send(src, dst, send_sem, recv_sem, target):
        copy = pltpu.make_async_remote_copy(
            src_ref=src,
            dst_ref=dst,
            send_sem=send_sem,
            recv_sem=recv_sem,
            device_id=target,
            device_id_type=MESH,
        )
        copy.start()
        pending.append(copy)
        return copy

    y_copies = []
    for c in range(count):
        arriving = []
        for d in list(range(1, rows)) + [0]:
            dest = lax.rem(row + d, rows)

            def y_step(a, carry, d=d, dest=dest):
                k = dest * kyd + a
                for t in range(td):
                    total = jnp.zeros((kx, 128), F32)
                    for y in range(yd):
                        total += tab_y[k, y0 + y] * sect[y * td + t]
                        total += tab_y[ky_all + k, y0 + y] * sect_s[y * td + t]
                    if d == 0:
                        y_recv[row, a, t] = total.astype(BF16)
                    else:
                        y_send[d - 1, a, t] = total.astype(BF16)
                return carry

            lax.fori_loop(c * span, (c + 1) * span, y_step, 0)
            if d > 0:
                arriving.append(
                    send(
                        y_send.at[d - 1, part[c]],
                        y_recv.at[row, part[c]],
                        ys_sem.at[d - 1, c],
                        yr_sem.at[d - 1, c],
                        {"row": dest},
                    )
                )
        y_copies.append(arriving)

    f_copy = send(field, f_all.at[:, mine, :], fs_sem, fr_sem, {"chan": 1 - chan})
    f_copy.wait_recv()

    eye = lax.broadcasted_iota(jnp.int32, (half, half), 0) == lax.broadcasted_iota(
        jnp.int32, (half, half), 1
    )
    column = jnp.sum(jnp.where(eye, bias[...], 0.0), axis=1, keepdims=True)

    def conv_step(i, carry):
        conv[i] = jnp.dot(conv_w[...], f_all[i], preferred_element_type=F32) + column
        return carry

    lax.fori_loop(0, yd * td, conv_step, 0)

    t_copies, c_copies, m_copies, b_copies = [], [], [], []

    def time_part(c):
        for copy in y_copies[c]:
            copy.wait_recv()

        def t_step(a, carry):
            parts = []
            for t in range(td):
                total = y_recv[0, a, t].astype(F32)
                for r in range(1, rows):
                    total += y_recv[r, a, t].astype(F32)
                parts.append((total, swap_halves(total) * sgn_f))
            for d in range(slabs):
                dest = lax.rem(tm + d, slabs)
                for b in range(ktd):
                    k = dest * ktd + b
                    value = jnp.zeros((kx, 128), F32)
                    for t in range(td):
                        value += tab_t[k, t0 + t] * parts[t][0]
                        value += tab_t[kt_all + k, t0 + t] * parts[t][1]
                    if d == 0:
                        own_kt[a, b] = value
                    else:
                        t_send[d - 1, a, b] = value.astype(BF16)
            return carry

        lax.fori_loop(c * span, (c + 1) * span, t_step, 0)
        t_copies.append(
            [
                send(
                    t_send.at[d - 1, part[c]],
                    t_recv.at[d - 1, part[c]],
                    ts_sem.at[d - 1, c],
                    tr_sem.at[d - 1, c],
                    {"tm": lax.rem(tm + d, slabs)},
                )
                for d in range(1, slabs)
            ]
        )

    def coef_part(c):
        for copy in t_copies[c]:
            copy.wait_recv()

        def c_step(a, carry):
            for b in range(ktd):
                value = own_kt[a, b]
                for d in range(1, slabs):
                    value += t_recv[d - 1, a, b].astype(F32)
                coef[chan, a, b] = value.astype(BF16)
            return carry

        lax.fori_loop(c * span, (c + 1) * span, c_step, 0)
        c_copies.append(
            send(
                coef.at[chan, part[c]],
                coef.at[chan, part[c]],
                cs_sem.at[c],
                cr_sem.at[c],
                {"chan": 1 - chan},
            )
        )

    group = 8 * 2 * half
    sub = lax.broadcasted_iota(jnp.int32, (8, 128), 0)
    zero = jnp.zeros((8, 128), F32)

    def mix_part(c):
        c_copies[c].wait_recv()
        w_copies[c].wait()

        def mix_step(i, carry):
            a, b = c * span + i // ktd, lax.rem(i, ktd)
            left = coef[0, a, b].astype(F32)
            right = coef[1, a, b].astype(F32)
            re = jnp.where(low, left, swap_halves(right))
            im = jnp.where(low, swap_halves(left), right)
            pieces = []
            for g in range(0, kx // 8, 2):
                first, second = slice(8 * g, 8 * g + 8), slice(8 * g + 8, 8 * g + 16)
                lhs = jnp.concatenate(
                    [
                        jnp.concatenate([re[first], zero], axis=1),
                        jnp.concatenate([im[first], zero], axis=1),
                        jnp.concatenate([zero, re[second]], axis=1),
                        jnp.concatenate([zero, im[second]], axis=1),
                    ],
                    axis=0,
                ).astype(BF16)
                rhs = jnp.concatenate(
                    [
                        w_all[b, a, g * group : (g + 1) * group, :],
                        w_all[b, a, (g + 1) * group : (g + 2) * group, :],
                    ],
                    axis=1,
                )
                result = lax.dot_general(
                    lhs, rhs, (((1,), (1,)), ((), ())), preferred_element_type=F32
                )
                for h in range(2):
                    by_part = []
                    for p in range(2):
                        tile = result[16 * h + 8 * p : 16 * h + 8 * p + 8]
                        total = tile[:, :128]
                        for m in range(1, 8):
                            total = jnp.where(sub == m, tile[:, 128 * m : 128 * m + 128], total)
                        by_part.append(total)
                    turned = swap_halves(by_part[1])
                    pieces.append(by_part[0] + jnp.where(low8, -turned, turned))
            modes[a, tm * ktd + b] = jnp.concatenate(pieces, axis=0).astype(BF16)
            return carry

        lax.fori_loop(0, span * ktd, mix_step, 0)
        own = pl.ds(tm * ktd, ktd)
        m_copies.append(
            [
                send(
                    modes.at[part[c], own],
                    modes.at[part[c], own],
                    ms_sem.at[d - 1, c],
                    mr_sem.at[d - 1, c],
                    {"tm": lax.rem(tm + d, slabs)},
                )
                for d in range(1, slabs)
            ]
        )

    def back_part(c):
        for copy in m_copies[c]:
            copy.wait_recv()

        def bt_step(a, carry):
            totals = [jnp.zeros((kx, 128), F32) for _ in range(td)]
            for k in range(kt_all):
                value = modes[a, k].astype(F32)
                turned = swap_halves(value) * sgn_b
                for t in range(td):
                    totals[t] += tab_t[k, t0 + t] * value + tab_t[kt_all + k, t0 + t] * turned
            for t in range(td):
                back[row, a, t] = totals[t].astype(BF16)
            return carry

        lax.fori_loop(c * span, (c + 1) * span, bt_step, 0)
        b_copies.append(
            [
                send(
                    back.at[row, part[c]],
                    back.at[row, part[c]],
                    bs_sem.at[d - 1, c],
                    br_sem.at[d - 1, c],
                    {"row": lax.rem(row + d, rows)},
                )
                for d in range(1, rows)
            ]
        )

    for c in range(count + 1):
        if c < count:
            time_part(c)
        if c > 0:
            mix_part(c - 1)
        if c < count:
            coef_part(c)
        if c > 0:
            back_part(c - 1)

    for c in range(count):
        for copy in b_copies[c]:
            copy.wait_recv()

        def by_step(t, carry, c=c):
            if c == 0:
                totals = [jnp.zeros((kx, 128), F32) for _ in range(yd)]
            else:
                totals = [acc[y * td + t] for y in range(yd)]
            for source in range(rows):
                for a in range(c * span, (c + 1) * span):
                    k = source * kyd + a
                    value = back[source, a, t].astype(F32)
                    turned = swap_halves(value) * sgn_b
                    for y in range(yd):
                        totals[y] += (
                            tab_y[k, y0 + y] * value + tab_y[ky_all + k, y0 + y] * turned
                        )
            for y in range(yd):
                acc[y * td + t] = totals[y]
            return carry

        lax.fori_loop(0, td, by_step, 0)

    def out_step(i, carry):
        first, second = acc[2 * i], acc[2 * i + 1]
        both = jnp.concatenate(
            [
                jnp.where(low, first, swap_halves(second)),
                jnp.where(low, swap_halves(first), second),
            ],
            axis=0,
        )
        spectral = jnp.dot(both.T.astype(BF16), x_inv[...], preferred_element_type=F32)
        value = spectral + conv[pl.ds(2 * i, 2)].reshape(2 * half, 128)
        value = 0.5 * value * (1.0 + lax.erf(value * np.float32(1.0 / np.sqrt(2.0))))
        out[pl.ds(2 * i, 2)] = value.astype(BF16).reshape(2, half, 128)
        return carry

    lax.fori_loop(0, yd * td // 2, out_step, 0)
    for copy in pending:
        copy.wait_send()


def body(field_in, spectral_weight, conv_weight, conv_bias):
    yd, td, half, nx = field_in.shape
    ktd, kyd, kx = spectral_weight.shape[:3]
    out_c, in_c = spectral_weight.shape[4:]
    rows, slabs = lax.axis_size("row"), lax.axis_size("tm")
    ny, nt = yd * rows, td * slabs
    ky_all, kt_all = kyd * rows, ktd * slabs

    turn_x = angles(np.arange(kx), np.arange(nx), nx)
    x_fwd = jnp.asarray(np.concatenate([np.cos(turn_x), -np.sin(turn_x)], axis=0), BF16)
    scale = (np.where(np.arange(kx) == 0, 1.0, 2.0) / (nx * ny * nt))[:, None]
    x_inv = jnp.asarray(
        np.concatenate([np.cos(turn_x) * scale, -np.sin(turn_x) * scale], axis=0), BF16
    )
    turn_y = angles(signed(ky_all), np.arange(ny), ny)
    tab_y = jnp.asarray(np.concatenate([np.cos(turn_y), np.sin(turn_y)], axis=0), F32)
    turn_t = angles(signed(kt_all), np.arange(nt), nt)
    tab_t = jnp.asarray(np.concatenate([np.cos(turn_t), np.sin(turn_t)], axis=0), F32)

    parts = min(4, kyd)
    dims = (rows, slabs, yd, td, kyd, ktd, kx, parts)
    vmem = pl.BlockSpec(memory_space=pltpu.VMEM)
    smem = pl.BlockSpec(memory_space=pltpu.SMEM)
    hbm = pl.BlockSpec(memory_space=pl.ANY)
    dma = pltpu.SemaphoreType.DMA
    tile = (kx, 128)
    result = pl.pallas_call(
        functools.partial(kernel, dims),
        out_shape=jax.ShapeDtypeStruct((yd * td, half, nx), BF16),
        in_specs=[hbm, hbm, vmem, vmem, vmem, vmem, smem, smem],
        out_specs=vmem,
        scratch_shapes=[
            pltpu.VMEM((ktd, kyd, kx * 2 * out_c, in_c), BF16),
            pltpu.VMEM((yd * td, in_c, nx), BF16),
            pltpu.VMEM((yd * td,) + tile, F32),
            pltpu.VMEM((yd * td,) + tile, F32),
            pltpu.VMEM((rows - 1, kyd, td) + tile, BF16),
            pltpu.VMEM((rows, kyd, td) + tile, BF16),
            pltpu.VMEM((kyd, ktd) + tile, F32),
            pltpu.VMEM((slabs - 1, kyd, ktd) + tile, BF16),
            pltpu.VMEM((slabs - 1, kyd, ktd) + tile, BF16),
            pltpu.VMEM((2, kyd, ktd) + tile, BF16),
            pltpu.VMEM((kyd, kt_all) + tile, BF16),
            pltpu.VMEM((rows, kyd, td) + tile, BF16),
            pltpu.VMEM((yd * td,) + tile, F32),
            pltpu.VMEM((yd * td, out_c, nx), F32),
            dma((parts,)),
            dma,
            dma,
            dma,
            dma((rows - 1, parts)),
            dma((rows - 1, parts)),
            dma((slabs - 1, parts)),
            dma((slabs - 1, parts)),
            dma((parts,)),
            dma((parts,)),
            dma((slabs - 1, parts)),
            dma((slabs - 1, parts)),
            dma((rows - 1, parts)),
            dma((rows - 1, parts)),
        ],
        compiler_params=pltpu.CompilerParams(
            collective_id=0, has_side_effects=True, vmem_limit_bytes=56 * 1024 * 1024
        ),
    )(
        field_in.reshape(yd * td, half, nx),
        spectral_weight.reshape(ktd, kyd, kx * 2 * out_c, in_c),
        conv_weight,
        conv_bias[None, :],
        x_fwd,
        x_inv,
        tab_y,
        tab_t,
    )
    return result.reshape(yd, td, half, nx)


def solution(mesh):
    return jax.shard_map(
        body,
        mesh=mesh,
        in_specs=(
            P(("groups", "row"), "tm", "chan", None),
            P("tm", "row", None, None, "chan", None),
            P("chan", None),
            P("chan"),
        ),
        out_specs=P(("groups", "row"), "tm", "chan", None),
        check_vma=False,
    )
```

time: 106 us -> 81.8 us (0.77)
  the two profiles are of different devices: /device:TPU:25 before, /device:TPU:0 now
where the time goes in v1:
time: 81.8 us; the launch traced here: 81.5 us
  Pallas kernels  79.6 us (97%)
  local copies, waits for them, and re-layouts  1.87 us (2%)
    pallas_call x1, Pallas kernels, body(): pl.pallas_call(functools.partial(kernel, dims), out_shape=jax.ShapeDtypeS...  79.6 us
    unnamed x1, local copies, waits for them, and re-layouts  1.87 us

profile of v1, /device:TPU:0, one launch (start us, length us, event | category | flops | bytes accessed | tf_op | source)
XLA Modules:
  0.0 81.5 jit_solution(6877198571994960725)
XLA Ops:
  0.0 79.6 %shard_map.82 = bf16[32,64,128]{2,1,0:T(8,128)(2,1)} custom-call(bf16[32,64,128]{2,1,0:T(8,128)(2,1)} %bitcast.6, bf16[4,8,4096,128]{3,2,1,0:T(8,128)(2,1)} %bitcast.4, bf16[64,128]{1,0:T(8,128)(2,1)} %conv_w.1, f32[1,64]{1,0:T(1,128)} %bitcast.7, bf16[64,128]{1,0:T(8,128)(2,1)} %constant.8.clone.x_fwd, bf16[64,128]{1,0:T(8,128)(2,1)} %constant.9.clone.x_inv, ...), custom_call_target="tpu_custom_call" | custom-call | tf_op jit(solution)/shard_map/pallas_call | solution.py:422
  79.6 1.9 %copy.10 = bf16[8,4,64,128]{3,2,1,0:T(8,128)(2,1)} copy(bf16[8,4,64,128]{3,2,1,0:T(8,128)(2,1)} %bitcast.5) | data formatting | bytes 1048576

commit v2 on v1

--- a/solution.py
+++ b/solution.py
@@ -118,7 +118,7 @@
         sect_s[2 * i + 1] = swap_halves(second) * sgn_f
         return carry
 
-    lax.fori_loop(0, yd * td // 2, x_step, 0)
+    lax.fori_loop(0, yd * td // 2, x_step, 0, unroll=4)
 
     pl.semaphore_wait(barrier, rows - 1 + slabs - 1 + 1)
     pending = []
@@ -180,7 +180,7 @@
         conv[i] = jnp.dot(conv_w[...], f_all[i], preferred_element_type=F32) + column
         return carry
 
-    lax.fori_loop(0, yd * td, conv_step, 0)
+    lax.fori_loop(0, yd * td, conv_step, 0, unroll=4)
 
     t_copies, c_copies, m_copies, b_copies = [], [], [], []
 
@@ -295,7 +295,7 @@
             modes[a, tm * ktd + b] = jnp.concatenate(pieces, axis=0).astype(BF16)
             return carry
 
-        lax.fori_loop(0, span * ktd, mix_step, 0)
+        lax.fori_loop(0, span * ktd, mix_step, 0, unroll=2)
         own = pl.ds(tm * ktd, ktd)
         m_copies.append(
             [
@@ -388,7 +388,7 @@
         out[pl.ds(2 * i, 2)] = value.astype(BF16).reshape(2, half, 128)
         return carry
 
-    lax.fori_loop(0, yd * td // 2, out_step, 0)
+    lax.fori_loop(0, yd * td // 2, out_step, 0, unroll=4)
     for copy in pending:
         copy.wait_send()
 

time: 81.8 us -> 71.3 us (0.87)
  Pallas kernels: 79.6 us -> 69.1 us
    pallas_call x1, Pallas kernels: 79.6 us -> 69.1 us  [body(): pl.pallas_call(functools.partial(kernel, dims), out_shape=jax.ShapeDtypeS...]
where the time goes in v2:
time: 71.3 us; the launch traced here: 71 us
  Pallas kernels  69.1 us (97%)
  local copies, waits for them, and re-layouts  1.87 us (3%)
    pallas_call x1, Pallas kernels, body(): pl.pallas_call(functools.partial(kernel, dims), out_shape=jax.ShapeDtypeS...  69.1 us
    unnamed x1, local copies, waits for them, and re-layouts  1.87 us

profile of v2, /device:TPU:0, one launch (start us, length us, event | category | flops | bytes accessed | tf_op | source)
XLA Modules:
  0.0 71.0 jit_solution(5143439538788751689)
XLA Ops:
  0.0 69.1 %shard_map.82 = bf16[32,64,128]{2,1,0:T(8,128)(2,1)} custom-call(bf16[32,64,128]{2,1,0:T(8,128)(2,1)} %bitcast.6, bf16[4,8,4096,128]{3,2,1,0:T(8,128)(2,1)} %bitcast.4, bf16[64,128]{1,0:T(8,128)(2,1)} %conv_w.1, f32[1,64]{1,0:T(1,128)} %bitcast.7, bf16[64,128]{1,0:T(8,128)(2,1)} %constant.8.clone.x_fwd, bf16[64,128]{1,0:T(8,128)(2,1)} %constant.9.clone.x_inv, ...), custom_call_target="tpu_custom_call" | custom-call | tf_op jit(solution)/shard_map/pallas_call | solution.py:422
  69.1 1.9 %copy.10 = bf16[8,4,64,128]{3,2,1,0:T(8,128)(2,1)} copy(bf16[8,4,64,128]{3,2,1,0:T(8,128)(2,1)} %bitcast.5) | data formatting | bytes 1048576
